TPU v7x, 32 devices: a whole 2x2x4 slice. The times are simulated.
32 devices in a mesh: groups: 2 (over x), gx: 16 (over z, y, core).
Axes of the slice: x: 2, y: 2, z: 4, core: 2. Of those that a mesh axis runs over, the one named last changes fastest.
Arguments:
- point_attributes: bfloat16 [16384, 128], P(('groups', 'gx')), parts along dimension 0, may hold values from -6 to 6
- kernel_matrices: bfloat16 [27, 128, 128], replicated, may hold values from -0.109375 to 0.109375
- cotangent_of_sum: bfloat16 [16384, 128], P(('groups', 'gx')), parts along dimension 0, may hold values from -6 to 6
- alive_point_counts: int32 [32], P(('groups', 'gx')), parts along dimension 0, may hold values from 64 to 512, as said below
- gather_lookup_plan: int32 [27, 16384], P(None, ('groups', 'gx')), parts along dimension 1, may hold values from -1 to 767, as said below
- export_point_lists: int32 [32, 4, 64], P(('groups', 'gx')), parts along dimension 0, may hold values from 0 to 511, as said below
Outputs:
- layer_result_vectors: bfloat16 [16384, 128], P(('groups', 'gx')), parts along dimension 0
- input_derivative: bfloat16 [16384, 128], P(('groups', 'gx')), parts along dimension 0
- grad_weight: float32 [54, 128, 128], P('groups'), parts along dimension 0
There are 2 independent parts, one for each index of `groups`. A program takes and returns all parts, laid end to end along the dimension named above; an argument that names none is the same for every part. Nothing has to cross between parts.
Inputs may be any that keep to these rules, and one draw needn't show every extreme that they name: `alive_point_counts`: some owner holds 512 live sites and some holds 64. `export_point_lists`: every entry names a live site of the sending owner; each side's list holds 64 entries, repeats allowed. `gather_lookup_plan`: -1 means no neighbour; the middle offset of a live site names the site itself; all entries of sites at or past the owner's count are -1; values under 512 name a live site of the same owner, the others a received row of site_table.
All inputs are finite; a program needn't handle non-finite values.
Results may differ from a plain program's by a relative error of at most 0.003.
Values may be sent and summed in bfloat16 or wider, within the bound.
A program may use at most 64 MiB of HBM per device.

v0:
```python
import math

import jax
import jax.numpy as jnp
from jax import lax
from jax.sharding import PartitionSpec as P


def passed_along(value, axis, steps):
    count = lax.axis_size(axis)
    initial, last = (max(0, -steps), min(count, count - steps))
    return lax.ppermute(value, axis, [(source, source + steps) for source in range(initial, last)])


def side_distance(slot_index):
    return (slot_index // 2 + 1) * (1 - 2 * (slot_index % 2))


def body(
    point_attributes,
    kernel_matrices,
    cotangent_of_sum,
    alive_point_counts,
    gather_lookup_plan,
    export_point_lists,
):
    site_total = point_attributes.shape[0]
    channel = point_attributes.shape[1]
    side_count = export_point_lists.shape[1]
    halo_size = export_point_lists.shape[2]
    offsets_all = kernel_matrices.shape[0]
    layer_span_range = math.gcd(site_total, 512)
    send_rows = export_point_lists[0]
    site_iota = jnp.arange(site_total, dtype=jnp.int32)
    send_picker = send_rows[:, :, None] == site_iota[None, None, :]
    outgoing = jnp.einsum(
        "khs,sc->khc",
        send_picker.astype(jnp.bfloat16),
        point_attributes,
        preferred_element_type=jnp.float32,
    ).astype(jnp.bfloat16)
    arrived = [None] * side_count
    for slot_index in range(side_count):
        arrived[slot_index] = passed_along(outgoing[slot_index], "gx", side_distance(slot_index))
    zero_row = site_total + side_count * halo_size
    table_rows = (zero_row + 1 + 127) // 128 * 128
    site_table = jnp.concatenate(
        [point_attributes]
        + arrived
        + [jnp.zeros((table_rows - zero_row, channel), point_attributes.dtype)],
        axis=0,
    )
    table_iota = jnp.arange(table_rows, dtype=jnp.int32)
    row_picks = jnp.where(gather_lookup_plan < 0, zero_row, gather_lookup_plan)
    filled_cell_markers = (site_iota < alive_point_counts[0]).astype(jnp.float32)[:, None]
    kernel_wide = kernel_matrices.astype(jnp.float32)

    def forward_rows():
        picker = (row_picks[:, :, None] == table_iota[None, None, :]).astype(jnp.bfloat16)
        gathered = jnp.einsum(
            "obr,rc->obc", picker, site_table, preferred_element_type=jnp.float32
        ).astype(jnp.bfloat16)
        linear_response = jnp.einsum(
            "obc,ocd->bd", gathered, kernel_matrices, preferred_element_type=jnp.float32
        )
        own_rows = point_attributes.astype(jnp.float32)
        grad_rows = cotangent_of_sum.astype(jnp.float32)
        logistic_multiplier = jax.nn.sigmoid(linear_response)
        new_rows = (
            filled_cell_markers * (own_rows + linear_response * logistic_multiplier)
        ).astype(jnp.bfloat16)
        linear_response_derivative = (
            filled_cell_markers
            * grad_rows
            * logistic_multiplier
            * (1.0 + linear_response * (1.0 - logistic_multiplier))
        ).astype(jnp.bfloat16)
        return (picker, gathered, new_rows, linear_response_derivative)

    block_limit = site_total // layer_span_range
    table_start = jnp.zeros((table_rows, channel), jnp.float32)
    weight_start = jnp.zeros((offsets_all, channel, channel), jnp.float32)

    def block_update(block_number, carried):
        layer_result_vectors, table_grad, weight_grad = carried
        picker, gathered, new_rows, linear_response_derivative = forward_rows()
        weight_grad = weight_grad + jnp.einsum(
            "obc,bd->ocd", gathered, linear_response_derivative, preferred_element_type=jnp.float32
        )
        collected = jnp.einsum(
            "obr,bd->ord", picker, linear_response_derivative, preferred_element_type=jnp.float32
        )
        table_grad = table_grad + jnp.einsum(
            "ord,ocd->rc", collected, kernel_wide, precision=lax.Precision.HIGHEST
        )
        layer_result_vectors = new_rows
        return (layer_result_vectors, table_grad, weight_grad)

    layer_result_vectors, table_grad, weight_grad = lax.fori_loop(
        0, block_limit, block_update, (jnp.zeros_like(point_attributes), table_start, weight_start)
    )
    grad_weight = lax.psum(weight_grad, "gx")
    parts = [
        table_grad[site_total + slot_index * halo_size : site_total + (slot_index + 1) * halo_size]
        for slot_index in range(side_count)
    ]
    backs = [None] * side_count
    for slot_index in range(side_count):
        backs[slot_index] = passed_along(
            parts[slot_index].astype(jnp.bfloat16), "gx", -side_distance(slot_index)
        ).astype(jnp.float32)
    returned_all = jnp.stack(backs)
    scattered = jnp.einsum(
        "khs,khc->sc",
        send_picker.astype(jnp.float32),
        returned_all,
        precision=lax.Precision.HIGHEST,
    )
    adjacent_accumulated = (
        cotangent_of_sum.astype(jnp.float32) + table_grad[:site_total] + scattered
    )
    input_derivative = (filled_cell_markers * adjacent_accumulated).astype(jnp.bfloat16)
    return (layer_result_vectors, input_derivative, grad_weight)


def solution(mesh):
    return jax.shard_map(
        body,
        mesh=mesh,
        in_specs=(
            P(("groups", "gx"), None),
            P(),
            P(("groups", "gx"), None),
            P(("groups", "gx")),
            P(None, ("groups", "gx")),
            P(("groups", "gx"), None, None),
        ),
        out_specs=(P(("groups", "gx"), None), P(("groups", "gx"), None), P("groups", None, None)),
        check_vma=False,
    )
```

profile of v0, /device:TPU:1, one launch (start us, length us, event | category | flops | bytes accessed | tf_op | source)
XLA Modules:
  0.0 163.0 jit_solution(2213301704559446713)
XLA Ops:
  7.2 0.0 copy-start
  7.2 0.0 all-reduce.2.cloned.1.call-start
  7.2 1.3 convolution_convert_fusion
  8.5 1.3 collective-permute-start.3
  9.8 4.6 %collective-permute-start.2 = (bf16[64,128]{1,0:T(8,128)(2,1)S(1)}, bf16[64,128]{1,0:T(8,128)(2,1)S(1)}, u32[]{:S(2)}, u32[]{:S(2)}) collective-permute-start(bf16[64,128]{1,0:T(8,128)(2,1)S(1)} %get-tuple-element.31), channel_id=1, source_target_pairs={{0,2},{1,3},{2,4},{3,5},{4,6},{5,7},{6,8},{7,9},{8,10},{9,11},{10,... | collective-permute-start | bytes 49160 | tf_op jit(solution)/shard_map/ppermute | solution.py:12
  14.4 2.9 %collective-permute-start.1 = (bf16[64,128]{1,0:T(8,128)(2,1)S(1)}, bf16[64,128]{1,0:T(8,128)(2,1)S(1)}, u32[]{:S(2)}, u32[]{:S(2)}) collective-permute-start(bf16[64,128]{1,0:T(8,128)(2,1)S(1)} %get-tuple-element.32), channel_id=1, source_target_pairs={{1,0},{2,1},{3,2},{4,3},{5,4},{6,5},{7,6},{8,7},{9,8},{10,9},{11,1... | collective-permute-start | bytes 49160 | tf_op jit(solution)/shard_map/ppermute | solution.py:12
  17.3 4.4 %collective-permute-start = (bf16[64,128]{1,0:T(8,128)(2,1)S(1)}, bf16[64,128]{1,0:T(8,128)(2,1)S(1)}, u32[]{:S(2)}, u32[]{:S(2)}) collective-permute-start(bf16[64,128]{1,0:T(8,128)(2,1)S(1)} %get-tuple-element.33), channel_id=1, source_target_pairs={{0,1},{1,2},{2,3},{3,4},{4,5},{5,6},{6,7},{7,8},{8,9},{9,10},{10,1... | collective-permute-start | bytes 49160 | tf_op jit(solution)/shard_map/ppermute | solution.py:12
  21.7 0.9 constant_dynamic-update-slice_fusion.4
  23.3 0.8 compare_select_fusion
  24.2 0.0 collective-permute-done
  24.2 0.0 collective-permute-done.1
  24.2 0.0 collective-permute-done.2
  24.2 0.0 collective-permute-done.3
  24.3 0.0 copy-start.1
  24.3 0.0 copy-start.2
  24.3 10.6 %fusion.4 = bf16[27,512,128]{2,1,0:T(8,128)(2,1)S(1)} fusion(s32[27,512]{1,0:T(8,128)S(1)} %compare_select_fusion, bf16[896,128]{1,0:T(8,128)(2,1)S(1)} %broadcast_dynamic-update-slice_fusion), kind=kOutput, calls=%fused_computation.5 | convolution fusion | flops 3185049600 | bytes 3823616 | tf_op jit(solution)/shard_map/while/body/eval_jaxpr/obr,rc->obc/dot_general | solution.py:60
  34.9 1.8 %multiply_convert_fusion = (bf16[512,128]{1,0:T(8,128)(2,1)}, f32[512,128]{1,0:T(8,128)S(1)}) fusion(bf16[512,128]{1,0:T(8,128)(2,1)S(1)} %copy-done.1, f32[512]{0:T(512)S(1)} %fusion.25, bf16[27,512,128]{2,1,0:T(8,128)(2,1)S(1)} %fusion.4, bf16[27,128,128]{2,1,0:T(8,128)(2,1)S(1)} %copy-done), kind=kOutput, calls=%fused_computation.19 | convolution fusion | flops 453509120 | bytes 4950016 | tf_op jit(solution)/shard_map/while/body/eval_jaxpr/obc,ocd->bd/dot_general | solution.py:63
  36.7 2.4 %fusion.14 = f32[27,128,128]{2,1,0:T(8,128)} fusion(bf16[27,512,128]{2,1,0:T(8,128)(2,1)S(1)} %fusion.4, bf16[512,128]{1,0:T(8,128)(2,1)S(1)} %copy-done.2, f32[512,128]{1,0:T(8,128)S(1)} %get-tuple-element.35, f32[512]{0:T(512)S(1)} %fusion.25), kind=kOutput, calls=%fused_computation.25 | convolution fusion | flops 453705728 | bytes 5703680 | tf_op jit(solution)/shard_map/while/body/eval_jaxpr/obc,bd->ocd/dot_general | solution.py:87
  39.1 18.1 %fusion = f32[27,896,128]{2,1,0:T(8,128)} fusion(s32[27,512]{1,0:T(8,128)S(1)} %compare_select_fusion, bf16[512,128]{1,0:T(8,128)(2,1)S(1)} %copy-done.2, f32[512,128]{1,0:T(8,128)S(1)} %get-tuple-element.35, f32[512]{0:T(512)S(1)} %fusion.25), kind=kOutput, calls=%fused_computation.1 | convolution fusion | flops 3184001024 | bytes 12836864 | tf_op jit(solution)/shard_map/while/body/eval_jaxpr/obr,bd->ord/dot_general | solution.py:90
  57.3 0.0 all-reduce.2.cloned.1.call-update
  57.3 8.6 %fusion.30 = (bf16[896,128]{1,0:T(8,128)(2,1)S(1)}, f32[896,128]{1,0:T(8,128)S(1)}) fusion(f32[27,896,128]{2,1,0:T(8,128)} %fusion, bf16[27,128,128]{2,1,0:T(8,128)(2,1)S(1)} %copy-done), kind=kOutput, calls=%fused_computation.50 | convolution fusion | flops 4756455424 | bytes 13959168 | tf_op jit(solution)/shard_map/while/body/eval_jaxpr/ord,ocd->rc/dot_general | solution.py:93
  65.9 1.9 %collective-permute-start.4 = (bf16[64,128]{1,0:T(8,128)(2,1)S(1)}, bf16[64,128]{1,0:T(8,128)(2,1)S(1)}, u32[]{:S(2)}, u32[]{:S(2)}) collective-permute-start(bf16[64,128]{1,0:T(8,128)(2,1)S(1)} %get-tuple-element.26), channel_id=1, source_target_pairs={{1,0},{2,1},{3,2},{4,3},{5,4},{6,5},{7,6},{8,7},{9,8},{10,9},{11,1... | collective-permute-start | bytes 49160 | tf_op jit(solution)/shard_map/ppermute | solution.py:12
  67.9 3.4 %collective-permute-start.7 = (bf16[64,128]{1,0:T(8,128)(2,1)S(1)}, bf16[64,128]{1,0:T(8,128)(2,1)S(1)}, u32[]{:S(2)}, u32[]{:S(2)}) collective-permute-start(bf16[64,128]{1,0:T(8,128)(2,1)S(1)} %get-tuple-element.27), channel_id=1, source_target_pairs={{0,2},{1,3},{2,4},{3,5},{4,6},{5,7},{6,8},{7,9},{8,10},{9,11},{10,... | collective-permute-start | bytes 49160 | tf_op jit(solution)/shard_map/ppermute | solution.py:12
  71.3 1.3 collective-permute-start.6
  72.6 5.5 %collective-permute-start.5 = (bf16[64,128]{1,0:T(8,128)(2,1)S(1)}, bf16[64,128]{1,0:T(8,128)(2,1)S(1)}, u32[]{:S(2)}, u32[]{:S(2)}) collective-permute-start(bf16[64,128]{1,0:T(8,128)(2,1)S(1)} %get-tuple-element.29), channel_id=1, source_target_pairs={{0,1},{1,2},{2,3},{3,4},{4,5},{5,6},{6,7},{7,8},{8,9},{9,10},{10,1... | collective-permute-start | bytes 49160 | tf_op jit(solution)/shard_map/ppermute | solution.py:12
  78.1 0.0 collective-permute-done.4
  78.1 0.0 collective-permute-done.7
  78.1 0.0 collective-permute-done.6
  78.1 0.8 collective-permute-done.5
  78.9 1.1 fusion.7
  80.0 73.3 %all-reduce.2.cloned.1.call-done = f32[27,128,128]{2,1,0:T(8,128)} async-done(((f32[27,128,128]{2,1,0:T(8,128)}), f32[27,128,128]{2,1,0:T(8,128)}) %all-reduce.2.cloned.1.call-update) | async-done | bytes 1769488 | tf_op jit(solution)/shard_map/psum | solution.py:102
  153.3 2.9 %copy.18 = f32[27,128,128]{2,1,0:T(8,128)} copy(f32[27,128,128]{2,1,0:T(8,128)} %all-reduce.2.cloned.1.call-done) | data formatting | bytes 3538944
  (13 shorter events, 0.1 us)
Async XLA Ops:
  7.2 27.8 %copy-start = (bf16[27,128,128]{2,1,0:T(8,128)(2,1)S(1)}, bf16[27,128,128]{2,1,0:T(8,128)(2,1)}, u32[]{:S(2)}) copy-start(bf16[27,128,128]{2,1,0:T(8,128)(2,1)} %param.7) | copy-start | bytes 2654212
  7.2 146.1 %all-reduce.2.cloned.1.call-start = ((), (), s32[]{:S(2)}) async-start(), calls=%async_computation | async-start | bytes 3538944 | tf_op jit(solution)/shard_map/psum | solution.py:102
  8.5 15.7 %collective-permute-start.3 = (bf16[64,128]{1,0:T(8,128)(2,1)S(1)}, bf16[64,128]{1,0:T(8,128)(2,1)S(1)}, u32[]{:S(2)}, u32[]{:S(2)}) collective-permute-start(bf16[64,128]{1,0:T(8,128)(2,1)S(1)} %get-tuple-element.30), channel_id=1, source_target_pairs={{2,0},{3,1},{4,2},{5,3},{6,4},{7,5},{8,6},{9,7},{10,8},{11,9},{12,... | collective-permute-start | bytes 49160 | tf_op jit(solution)/shard_map/ppermute | solution.py:12
  9.8 14.4 %collective-permute-start.2 = (bf16[64,128]{1,0:T(8,128)(2,1)S(1)}, bf16[64,128]{1,0:T(8,128)(2,1)S(1)}, u32[]{:S(2)}, u32[]{:S(2)}) collective-permute-start(bf16[64,128]{1,0:T(8,128)(2,1)S(1)} %get-tuple-element.31), channel_id=1, source_target_pairs={{0,2},{1,3},{2,4},{3,5},{4,6},{5,7},{6,8},{7,9},{8,10},{9,11},{10,... | collective-permute-start | bytes 49160 | tf_op jit(solution)/shard_map/ppermute | solution.py:12
  14.4 9.8 %collective-permute-start.1 = (bf16[64,128]{1,0:T(8,128)(2,1)S(1)}, bf16[64,128]{1,0:T(8,128)(2,1)S(1)}, u32[]{:S(2)}, u32[]{:S(2)}) collective-permute-start(bf16[64,128]{1,0:T(8,128)(2,1)S(1)} %get-tuple-element.32), channel_id=1, source_target_pairs={{1,0},{2,1},{3,2},{4,3},{5,4},{6,5},{7,6},{8,7},{9,8},{10,9},{11,1... | collective-permute-start | bytes 49160 | tf_op jit(solution)/shard_map/ppermute | solution.py:12
  17.3 6.9 %collective-permute-start = (bf16[64,128]{1,0:T(8,128)(2,1)S(1)}, bf16[64,128]{1,0:T(8,128)(2,1)S(1)}, u32[]{:S(2)}, u32[]{:S(2)}) collective-permute-start(bf16[64,128]{1,0:T(8,128)(2,1)S(1)} %get-tuple-element.33), channel_id=1, source_target_pairs={{0,1},{1,2},{2,3},{3,4},{4,5},{5,6},{6,7},{7,8},{8,9},{9,10},{10,1... | collective-permute-start | bytes 49160 | tf_op jit(solution)/shard_map/ppermute | solution.py:12
  24.3 10.7 %copy-start.1 = (bf16[512,128]{1,0:T(8,128)(2,1)S(1)}, bf16[512,128]{1,0:T(8,128)(2,1)}, u32[]{:S(2)}) copy-start(bf16[512,128]{1,0:T(8,128)(2,1)} %param.6) | copy-start | bytes 393220
  24.3 12.4 %copy-start.2 = (bf16[512,128]{1,0:T(8,128)(2,1)S(1)}, bf16[512,128]{1,0:T(8,128)(2,1)}, u32[]{:S(2)}) copy-start(bf16[512,128]{1,0:T(8,128)(2,1)} %param.8) | copy-start | bytes 393220
  57.3 21.6 %copy-start.3 = (s32[1,4,64]{2,1,0:T(4,128)S(1)}, s32[1,4,64]{2,1,0:T(4,128)}, u32[]{:S(2)}) copy-start(s32[1,4,64]{2,1,0:T(4,128)} %param.11) | copy-start | bytes 3076
  65.9 12.1 %collective-permute-start.4 = (bf16[64,128]{1,0:T(8,128)(2,1)S(1)}, bf16[64,128]{1,0:T(8,128)(2,1)S(1)}, u32[]{:S(2)}, u32[]{:S(2)}) collective-permute-start(bf16[64,128]{1,0:T(8,128)(2,1)S(1)} %get-tuple-element.26), channel_id=1, source_target_pairs={{1,0},{2,1},{3,2},{4,3},{5,4},{6,5},{7,6},{8,7},{9,8},{10,9},{11,1... | collective-permute-start | bytes 49160 | tf_op jit(solution)/shard_map/ppermute | solution.py:12
  67.9 10.2 %collective-permute-start.7 = (bf16[64,128]{1,0:T(8,128)(2,1)S(1)}, bf16[64,128]{1,0:T(8,128)(2,1)S(1)}, u32[]{:S(2)}, u32[]{:S(2)}) collective-permute-start(bf16[64,128]{1,0:T(8,128)(2,1)S(1)} %get-tuple-element.27), channel_id=1, source_target_pairs={{0,2},{1,3},{2,4},{3,5},{4,6},{5,7},{6,8},{7,9},{8,10},{9,11},{10,... | collective-permute-start | bytes 49160 | tf_op jit(solution)/shard_map/ppermute | solution.py:12
  71.3 6.8 %collective-permute-start.6 = (bf16[64,128]{1,0:T(8,128)(2,1)S(1)}, bf16[64,128]{1,0:T(8,128)(2,1)S(1)}, u32[]{:S(2)}, u32[]{:S(2)}) collective-permute-start(bf16[64,128]{1,0:T(8,128)(2,1)S(1)} %get-tuple-element.28), channel_id=1, source_target_pairs={{2,0},{3,1},{4,2},{5,3},{6,4},{7,5},{8,6},{9,7},{10,8},{11,9},{12,... | collective-permute-start | bytes 49160 | tf_op jit(solution)/shard_map/ppermute | solution.py:12
  72.6 6.3 %collective-permute-start.5 = (bf16[64,128]{1,0:T(8,128)(2,1)S(1)}, bf16[64,128]{1,0:T(8,128)(2,1)S(1)}, u32[]{:S(2)}, u32[]{:S(2)}) collective-permute-start(bf16[64,128]{1,0:T(8,128)(2,1)S(1)} %get-tuple-element.29), channel_id=1, source_target_pairs={{0,1},{1,2},{2,3},{3,4},{4,5},{5,6},{6,7},{7,8},{8,9},{9,10},{10,1... | collective-permute-start | bytes 49160 | tf_op jit(solution)/shard_map/ppermute | solution.py:12
Sparse Core Ops, SparseCore 0:
  57.4 95.8 all-reduce.1
where the time goes:
time: 165 us; the launch traced here: 163 us
  waiting for transfers between devices  74.1 us (45%)
  matrix products  43.9 us (27%)
  starting transfers between devices  25.3 us (15%)
  between operations  14.9 us (9%)
  local copies, waits for them, and re-layouts  3.88 us (2%)
    psum x1, waiting for transfers between devices, body(): grad_weight = lax.psum(weight_grad, 'gx')  73.3 us
    ppermute x8, starting transfers between devices, passed_along(): lax.ppermute(value, axis, [(source, source + steps) for source in range(i...  25.3 us
    dot_general x1, matrix products, block_update(): jnp.einsum('obr,bd->ord', picker, linear_response_derivative, preferred_e...  18.1 us
    dot_general x1, matrix products, forward_rows(): jnp.einsum('obr,rc->obc', picker, site_table, preferred_element_type=jnp....  10.6 us
    dot_general x1, matrix products, block_update(): jnp.einsum('ord,ocd->rc', collected, kernel_wide, precision=lax.Precision...  8.62 us
    unnamed x14, local copies, waits for them, and re-layouts  3.85 us
  transfers between devices with their start and end apart: 9, of which 2 were waited for; matrix products, arithmetic and copies ran while one was open for 7% of the time, Pallas kernels for 0%

commit v1 on v0

v1 whole, which is shorter than its diff:
```python
import functools

import jax
import jax.numpy as jnp
from jax import lax
from jax.experimental import pallas as pl
from jax.experimental.pallas import tpu as pltpu
from jax.sharding import PartitionSpec as P

BF = jnp.bfloat16
F32 = jnp.float32
MESH = pl.DeviceIdType.MESH
PIECES = 2
GROUP = 4


def side_distance(slot_index):
    return (slot_index // 2 + 1) * (1 - 2 * (slot_index % 2))


def grid_of(devices):
    chips = devices // 2
    near = 1
    while (near * 2) ** 2 <= chips and chips % (near * 2) == 0:
        near *= 2
    return near, chips // near


def rows_each(devices, padded_rows):
    share = -(-padded_rows // (PIECES * devices))
    return -(-share // 16) * 16


def kernel(
    n, r, offsets, padded,
    x_ref, w_hbm, cot_ref, cnt_ref, idx_ref, exp_ref,
    out_ref, din_ref, gw_ref,
    w_s, idx_s, t01, t2, idxb, lob, lo16, iota_s, g_s, acc, d_s, r1, s2, r2, b_s, s3, r3, og,
    hs, tacc, bs, br,
    w_sem, o_sem, hsem, hrem, bsem, brem,
    c1s, c1r, y1s, y1r, z1s, z1r, z2s, z2r, y2s, y2r, c2s, c2r,
):
    sites, ch = x_ref.shape
    sides, halo = exp_ref.shape[1], exp_ref.shape[2]
    near, far = grid_of(n)
    me = lax.axis_index("gx")
    c = lax.rem(me, 2)
    y = lax.rem(me // 2, near)
    z = me // (2 * near)
    quarter = far * r
    half = near * quarter
    low = sites // 2
    lo_rows = (sites + sides * halo) // 2

    def dev(cc, yy, zz):
        return {"gx": cc + 2 * (yy + near * zz)}

    def around(value, delta, size):
        return lax.rem(value + delta, size)

    core_peer = dev(1 - c, y, z)
    y_peers = [dev(c, around(y, k, near), z) for k in range(1, near)]
    z_peers = [dev(c, y, around(z, k, far)) for k in range(1, far)]
    fixed_peers = [core_peer] + y_peers + z_peers

    def exists(owner):
        return (owner >= 0) & (owner < n)

    barrier = pltpu.get_barrier_semaphore()
    for peer in fixed_peers:
        pl.semaphore_signal(barrier, inc=1, device_id=peer, device_id_type=MESH)
    for k in range(sides):
        owner = me + side_distance(k)

        @pl.when(exists(owner))
        def _(owner=owner):
            pl.semaphore_signal(barrier, inc=1, device_id={"gx": owner}, device_id_type=MESH)

    w_copy = pltpu.make_async_copy(w_hbm, w_s.at[pl.ds(0, offsets * ch)], w_sem)
    w_copy.start()
    w_s[pl.ds(offsets * ch, (padded - offsets) * ch), :] = jnp.zeros(
        ((padded - offsets) * ch, ch), BF
    )

    def export_picks(k):
        places = lax.broadcasted_iota(jnp.int32, (sites, halo), 0)
        return jnp.where(places == exp_ref[0, k : k + 1, :], 1.0, 0.0).astype(BF)

    for k in range(sides):
        hs[pl.ds(k * halo, halo), :] = lax.dot_general(
            export_picks(k), x_ref[...], (((0,), (0,)), ((), ())), preferred_element_type=F32
        ).astype(BF)

        @pl.when(jnp.logical_not(exists(me - side_distance(k))))
        def _(k=k):
            t2[pl.ds(k * halo, halo), :] = jnp.zeros((halo, ch), BF)

        @pl.when(jnp.logical_not(exists(me + side_distance(k))))
        def _(k=k):
            br[pl.ds(k * halo, halo), :] = jnp.zeros((halo, ch), BF)

    greeted = len(fixed_peers)
    for k in range(sides):
        greeted += jnp.where(exists(me + side_distance(k)), 1, 0)
    pl.semaphore_wait(barrier, greeted)

    def halo_copy(k):
        return pltpu.make_async_remote_copy(
            src_ref=hs.at[pl.ds(k * halo, halo)],
            dst_ref=t2.at[pl.ds(k * halo, halo)],
            send_sem=hsem.at[k],
            recv_sem=hrem.at[k],
            device_id={"gx": me + side_distance(k)},
            device_id_type=MESH,
        )

    def back_copy(k):
        return pltpu.make_async_remote_copy(
            src_ref=bs.at[pl.ds(k * halo, halo)],
            dst_ref=br.at[pl.ds(k * halo, halo)],
            send_sem=bsem.at[k],
            recv_sem=brem.at[k],
            device_id={"gx": me - side_distance(k)},
            device_id_type=MESH,
        )

    for k in range(sides):

        @pl.when(exists(me + side_distance(k)))
        def _(k=k):
            halo_copy(k).start()

    t01[:, pl.ds(0, ch)] = x_ref[pl.ds(0, low), :]
    t01[:, pl.ds(ch, ch)] = x_ref[pl.ds(low, low), :]
    idx_s[...] = jnp.full(idx_s.shape, -1.0, F32)
    idx_s[pl.ds(0, offsets), :] = idx_ref[...].astype(F32)
    rows = idx_s[...]
    lo_f = jnp.where(rows >= 2 * low, rows - 2 * low, jnp.where(rows >= low, rows - low, rows))
    lo_b = jnp.where(
        rows < 0, -1.0 * low + 1.0, jnp.where(rows >= lo_rows, rows - lo_rows, rows) - low / 2
    )
    rows_t = rows.T
    lo_t = lo_f.T
    for o in range(padded):
        idxb[o] = jnp.broadcast_to(rows_t[:, o : o + 1], (sites, ch))
        lob[o] = jnp.broadcast_to(lo_t[:, o : o + 1], (sites, ch)).astype(BF)
        lo16[o] = jnp.broadcast_to(lo_b[o : o + 1, :], (16, sites)).astype(BF)
    iota_s[...] = (
        lax.broadcasted_iota(jnp.int32, iota_s.shape, 0).astype(F32) - low / 2
    ).astype(BF)
    lanes = lax.broadcasted_iota(jnp.int32, (sites, ch), 1).astype(F32)
    lanes_a = lanes.astype(BF)
    lanes_b = (lanes + ch).astype(BF)
    one = jnp.ones((), BF)
    zero = jnp.zeros((), BF)

    def low_picks(o):
        lo = lob[o]
        return jnp.concatenate(
            [jnp.where(lo == lanes_a, one, zero), jnp.where(lo == lanes_b, one, zero)], axis=1
        )

    def own_rows(step, _):
        for i in range(GROUP):
            o = step * GROUP + i
            both = jnp.dot(low_picks(o), t01[...], preferred_element_type=F32)
            place = idxb[o]
            picked = jnp.where(
                place < low, both[:, :ch], jnp.where(place < 2 * low, both[:, ch:], 0.0)
            )
            g_s[:, pl.ds(pl.multiple_of(o * ch, ch), ch)] = picked.astype(BF)
        return 0

    lax.fori_loop(0, padded // GROUP, own_rows, 0)
    w_copy.wait()
    for k in range(sides):

        @pl.when(exists(me - side_distance(k)))
        def _(k=k):
            halo_copy(k).wait_recv()

    acc[...] = jnp.zeros_like(acc)

    def halo_rows(step, _):
        for i in range(GROUP):
            o = step * GROUP + i
            far_rows = jnp.dot(low_picks(o), t2[...], preferred_element_type=F32)
            where_o = pl.ds(pl.multiple_of(o * ch, ch), ch)
            g_s[:, where_o] = jnp.where(
                idxb[o] >= 2 * low, far_rows, g_s[:, where_o].astype(F32)
            ).astype(BF)
        span = pl.ds(pl.multiple_of(step * GROUP * ch, GROUP * ch), GROUP * ch)
        acc[...] += jnp.dot(g_s[:, span], w_s[span, :], preferred_element_type=F32)
        return 0

    lax.fori_loop(0, padded // GROUP, halo_rows, 0)

    live = jnp.where(
        lax.broadcasted_iota(jnp.int32, (sites, ch), 0) < cnt_ref[0], 1.0, 0.0
    )
    preact = acc[...]
    gate = jax.nn.sigmoid(preact)
    out_ref[...] = (live * (x_ref[...].astype(F32) + preact * gate)).astype(BF)
    pre_grad = (
        live * cot_ref[...].astype(F32) * gate * (1.0 + preact * (1.0 - gate))
    ).astype(BF)
    acc[...] = pre_grad.astype(F32)

    def weight_rows(step, _):
        span = pl.ds(pl.multiple_of(step * GROUP * ch, GROUP * ch), GROUP * ch)
        d_s[span, :] = lax.dot_general(
            g_s[:, span], acc[...].astype(BF), (((0,), (0,)), ((), ())),
            preferred_element_type=F32,
        )
        return 0

    piece = 2 * half
    extra = PIECES * piece - padded * ch
    if extra:
        d_s[pl.ds(padded * ch, extra), :] = jnp.zeros((extra, ch), F32)

    def remote(src, dst, send, recv, peer):
        return pltpu.make_async_remote_copy(
            src_ref=src, dst_ref=dst, send_sem=send, recv_sem=recv,
            device_id=peer, device_id_type=MESH,
        )

    def at(start, size):
        return pl.ds(pl.multiple_of(start, 16), size)

    def core_sum(p):
        return remote(
            d_s.at[at(p * piece + (1 - c) * half, half)], r1.at[at(p * half, half)],
            c1s.at[p], c1r.at[p], core_peer,
        )

    def y_sum(p, k):
        slot = p * (near - 1) + k
        part = at(slot * quarter, quarter)
        return remote(s2.at[part], r2.at[part], y1s.at[slot], y1r.at[slot], y_peers[k])

    def z_sum(p, k):
        slot = p * (far - 1) + k
        part = at(slot * r, r)
        return remote(s3.at[part], r3.at[part], z1s.at[slot], z1r.at[slot], z_peers[k])

    def z_share(p, k):
        slot = p * (far - 1) + k
        part = at(p * piece + c * half + y * quarter + z * r, r)
        return remote(og.at[part], og.at[part], z2s.at[slot], z2r.at[slot], z_peers[k])

    def y_share(p, k):
        slot = p * (near - 1) + k
        part = at(p * piece + c * half + y * quarter, quarter)
        return remote(og.at[part], og.at[part], y2s.at[slot], y2r.at[slot], y_peers[k])

    def core_share(p):
        part = at(p * piece + c * half, half)
        return remote(og.at[part], og.at[part], c2s.at[p], c2r.at[p], core_peer)

    def out_copy(p):
        part = pl.ds(p * piece, piece)
        return pltpu.make_async_copy(og.at[part], gw_ref.at[part], o_sem.at[p])

    def after_core(p):
        core_sum(p).wait_recv()
        for k in range(near - 1):
            yy = around(y, k + 1, near)
            s2[at((p * (near - 1) + k) * quarter, quarter), :] = (
                d_s[at(p * piece + c * half + yy * quarter, quarter), :]
                + r1[at(p * half + yy * quarter, quarter), :]
            ).astype(BF)
            y_sum(p, k).start()
        b_s[at(p * quarter, quarter), :] = (
            d_s[at(p * piece + c * half + y * quarter, quarter), :]
            + r1[at(p * half + y * quarter, quarter), :]
        )

    def after_y(p):
        for k in range(near - 1):
            y_sum(p, k).wait_recv()
        total = b_s[at(p * quarter, quarter), :]
        for k in range(near - 1):
            total += r2[at((p * (near - 1) + k) * quarter, quarter), :].astype(F32)
        b_s[at(p * quarter, quarter), :] = total
        for k in range(far - 1):
            zz = around(z, k + 1, far)
            s3[at((p * (far - 1) + k) * r, r), :] = b_s[at(p * quarter + zz * r, r), :].astype(BF)
            z_sum(p, k).start()

    def after_z(p):
        for k in range(far - 1):
            z_sum(p, k).wait_recv()
        total = b_s[at(p * quarter + z * r, r), :]
        for k in range(far - 1):
            total += r3[at((p * (far - 1) + k) * r, r), :].astype(F32)
        og[at(p * piece + c * half + y * quarter + z * r, r), :] = total.astype(BF)
        for k in range(far - 1):
            z_share(p, k).start()

    def after_z_share(p):
        for k in range(far - 1):
            z_share(p, k).wait_recv()
        for k in range(near - 1):
            y_share(p, k).start()

    def after_y_share(p):
        for k in range(near - 1):
            y_share(p, k).wait_recv()
        core_share(p).start()

    def after_core_share(p):
        core_share(p).wait_recv()
        out_copy(p).start()

    tacc[...] = jnp.zeros_like(tacc)

    def table_rows(step, _):
        span = pl.ds(pl.multiple_of(step * GROUP * ch, GROUP * ch), GROUP * ch)
        spread = lax.dot_general(
            acc[...].astype(BF), w_s[span, :], (((1,), (1,)), ((), ())),
            preferred_element_type=F32,
        )
        picks, parts = [], []
        for i in range(GROUP):
            o = step * GROUP + i
            upper = idxb[o] >= lo_rows
            term = spread[:, i * ch : (i + 1) * ch]
            parts.append(
                jnp.concatenate(
                    [jnp.where(upper, 0.0, term).astype(BF), jnp.where(upper, term, 0.0).astype(BF)],
                    axis=1,
                )
            )
            hit = iota_s[...].reshape(lo_rows // 16, 16, sites) == lo16[o][None]
            picks.append(jnp.where(hit, one, zero).reshape(lo_rows, sites))
        tacc[...] += jnp.dot(
            jnp.concatenate(picks, axis=1),
            jnp.concatenate(parts, axis=0),
            preferred_element_type=F32,
        )
        return 0

    steps = padded // GROUP
    first = -(-piece // (GROUP * ch))
    lax.fori_loop(0, min(first, steps), weight_rows, 0)
    core_sum(0).start()
    lax.fori_loop(min(first, steps), steps, weight_rows, 0)
    core_sum(1).start()
    lax.fori_loop(0, 2, table_rows, 0)
    after_core(0)
    after_core(1)
    lax.fori_loop(2, 4, table_rows, 0)
    after_y(0)
    lax.fori_loop(4, 6, table_rows, 0)
    after_y(1)
    lax.fori_loop(6, steps, table_rows, 0)
    bs[...] = tacc[pl.ds(lo_rows - sides * halo, sides * halo), pl.ds(ch, ch)].astype(BF)
    for k in range(sides):

        @pl.when(exists(me - side_distance(k)))
        def _(k=k):
            back_copy(k).start()

    after_z(0)
    after_z(1)
    after_z_share(0)
    for k in range(sides):

        @pl.when(exists(me + side_distance(k)))
        def _(k=k):
            back_copy(k).wait_recv()

    scattered = jnp.dot(export_picks(0), br[pl.ds(0, halo), :], preferred_element_type=F32)
    for k in range(1, sides):
        scattered += jnp.dot(
            export_picks(k), br[pl.ds(k * halo, halo), :], preferred_element_type=F32
        )
    own = jnp.concatenate(
        [tacc[:, pl.ds(0, ch)], tacc[pl.ds(0, sites - lo_rows), pl.ds(ch, ch)]], axis=0
    )
    din_ref[...] = (live * (cot_ref[...].astype(F32) + own + scattered)).astype(BF)
    after_z_share(1)
    after_y_share(0)
    after_y_share(1)
    after_core_share(0)
    after_core_share(1)

    for k in range(sides):

        @pl.when(exists(me + side_distance(k)))
        def _(k=k):
            halo_copy(k).wait_send()

        @pl.when(exists(me - side_distance(k)))
        def _(k=k):
            back_copy(k).wait_send()

    for p in range(PIECES):
        core_sum(p).wait_send()
        for k in range(near - 1):
            y_sum(p, k).wait_send()
            y_share(p, k).wait_send()
        for k in range(far - 1):
            z_sum(p, k).wait_send()
            z_share(p, k).wait_send()
        core_share(p).wait_send()
        out_copy(p).wait()


def body(x, w, cot, counts, plan, exports):
    n = lax.axis_size("gx")
    sites, ch = x.shape
    offsets = w.shape[0]
    padded = -(-offsets // GROUP) * GROUP
    sides, halo = exports.shape[1:]
    near, far = grid_of(n)
    r = rows_each(n, padded * ch)
    quarter = far * r
    half = near * quarter
    total = PIECES * 2 * half
    lo_rows = (sites + sides * halo) // 2
    vmem = pl.BlockSpec(memory_space=pltpu.VMEM)
    anyspace = pl.BlockSpec(memory_space=pl.ANY)
    smem = pl.BlockSpec(memory_space=pltpu.SMEM)
    dma = pltpu.SemaphoreType.DMA
    y_slots = max(1, PIECES * (near - 1))
    z_slots = max(1, PIECES * (far - 1))
    out, din, gw = pl.pallas_call(
        functools.partial(kernel, n, r, offsets, padded),
        out_shape=(
            jax.ShapeDtypeStruct((sites, ch), BF),
            jax.ShapeDtypeStruct((sites, ch), BF),
            jax.ShapeDtypeStruct((total, ch), BF),
        ),
        in_specs=[vmem, anyspace, vmem, smem, vmem, vmem],
        out_specs=(vmem, vmem, anyspace),
        scratch_shapes=[
            pltpu.VMEM((padded * ch, ch), BF),
            pltpu.VMEM((-(-padded // 8) * 8, sites), F32),
            pltpu.VMEM((sites // 2, 2 * ch), BF),
            pltpu.VMEM((sides * halo, ch), BF),
            pltpu.VMEM((padded, sites, ch), F32),
            pltpu.VMEM((padded, sites, ch), BF),
            pltpu.VMEM((padded, 16, sites), BF),
            pltpu.VMEM((lo_rows, sites), BF),
            pltpu.VMEM((sites, padded * ch), BF),
            pltpu.VMEM((sites, ch), F32),
            pltpu.VMEM((total, ch), F32),
            pltpu.VMEM((PIECES * half, ch), F32),
            pltpu.VMEM((y_slots * quarter, ch), BF),
            pltpu.VMEM((y_slots * quarter, ch), BF),
            pltpu.VMEM((PIECES * quarter, ch), F32),
            pltpu.VMEM((z_slots * r, ch), BF),
            pltpu.VMEM((z_slots * r, ch), BF),
            pltpu.VMEM((total, ch), BF),
            pltpu.VMEM((sides * halo, ch), BF),
            pltpu.VMEM((lo_rows, 2 * ch), F32),
            pltpu.VMEM((sides * halo, ch), BF),
            pltpu.VMEM((sides * halo, ch), BF),
            dma,
            dma((PIECES,)),
            dma((sides,)), dma((sides,)), dma((sides,)), dma((sides,)),
            dma((PIECES,)), dma((PIECES,)),
            dma((y_slots,)), dma((y_slots,)),
            dma((z_slots,)), dma((z_slots,)),
            dma((z_slots,)), dma((z_slots,)),
            dma((y_slots,)), dma((y_slots,)),
            dma((PIECES,)), dma((PIECES,)),
        ],
        compiler_params=pltpu.CompilerParams(
            collective_id=0, has_side_effects=True, vmem_limit_bytes=50 * 1024 * 1024
        ),
    )(x, w.reshape(offsets * ch, ch), cot, counts, plan, exports)
    grad_weight = gw[: offsets * ch].astype(F32).reshape(offsets, ch, ch)
    return out, din, grad_weight


def solution(mesh):
    return jax.shard_map(
        body,
        mesh=mesh,
        in_specs=(
            P(("groups", "gx"), None),
            P(),
            P(("groups", "gx"), None),
            P(("groups", "gx")),
            P(None, ("groups", "gx")),
            P(("groups", "gx"), None, None),
        ),
        out_specs=(P(("groups", "gx"), None), P(("groups", "gx"), None), P("groups", None, None)),
        check_vma=False,
    )
```

time: 165 us -> 53 us (0.32); the launches traced: 163 us -> 52.7 us
  waiting for transfers between devices: 74.1 us -> 0 us
  Pallas kernels: 0 us -> 44.1 us
  matrix products: 43.9 us -> 0 us
  starting transfers between devices: 25.3 us -> 0 us
  between operations: 14.9 us -> 1.31 us
  local copies, waits for them, and re-layouts: 3.88 us -> 5.86 us
    psum x1 -> x0, waiting for transfers between devices: 73.3 us -> none  [body(): grad_weight = lax.psum(weight_grad, 'gx')]
    pallas_call x0 -> x1, Pallas kernels: none -> 44.1 us  [body(): pl.pallas_call(functools.partial(kernel, n, r, offsets, padded), out_shap...]
    dot_general x7 -> x0, matrix products: 43.9 us -> none  [the longest x1 18.1 us: block_update(): jnp.einsum('obr,bd->ord', picker, linear_response_derivative, preferred_e...]
    ppermute x8 -> x0, starting transfers between devices: 25.3 us -> none  [passed_along(): lax.ppermute(value, axis, [(source, source + steps) for source in range(i...]
    unnamed x14 -> x12, local copies, waits for them, and re-layouts: 3.85 us -> 5.8 us
  transfers between devices with their start and end apart: 9 -> 0, of which waited for: 2 -> 0; matrix products, arithmetic and copies ran while one was open for 7% -> 0% of each run, Pallas kernels for 0% -> 0%
where the time goes in v1:
time: 53 us; the launch traced here: 52.7 us
  Pallas kernels  44.1 us (83%)
  local copies, waits for them, and re-layouts  5.86 us (11%)
  other arithmetic  1.41 us (3%)
  between operations  1.31 us (2%)
    pallas_call x1, Pallas kernels, body(): pl.pallas_call(functools.partial(kernel, n, r, offsets, padded), out_shap...  44.1 us
    unnamed x12, local copies, waits for them, and re-layouts  5.8 us
    reshape x1, other arithmetic, body(): grad_weight = gw[:offsets * ch].astype(F32).reshape(offsets, ch, ch)  1.41 us

profile of v1, /device:TPU:1, one launch (start us, length us, event | category | flops | bytes accessed | tf_op | source)
XLA Modules:
  0.0 52.7 jit_solution(10949488268513733932)
XLA Ops:
  1.3 0.0 copy-start
  1.3 1.2 %copy-done = bf16[27,128,128]{2,1,0:T(8,128)(2,1)S(1)} copy-done((bf16[27,128,128]{2,1,0:T(8,128)(2,1)S(1)}, bf16[27,128,128]{2,1,0:T(8,128)(2,1)}, u32[]{:S(2)}) %copy-start) | copy-done | bytes 884760
  2.4 0.0 copy-start.1
  2.4 0.9 %copy-done.1 = bf16[512,128]{1,0:T(8,128)(2,1)S(1)} copy-done((bf16[512,128]{1,0:T(8,128)(2,1)S(1)}, bf16[512,128]{1,0:T(8,128)(2,1)}, u32[]{:S(2)}) %copy-start.1) | copy-done | bytes 131096
  3.4 0.0 copy-start.2
  3.4 0.9 %copy-done.2 = bf16[512,128]{1,0:T(8,128)(2,1)S(1)} copy-done((bf16[512,128]{1,0:T(8,128)(2,1)S(1)}, bf16[512,128]{1,0:T(8,128)(2,1)}, u32[]{:S(2)}) %copy-start.2) | copy-done | bytes 131096
  4.3 0.0 copy-start.3
  4.3 0.8 %copy-done.3 = s32[27,512]{1,0:T(8,128)S(1)} copy-done((s32[27,512]{1,0:T(8,128)S(1)}, s32[27,512]{1,0:T(8,128)}, u32[]{:S(2)}) %copy-start.3) | copy-done | bytes 55320
  5.1 0.0 copy-start.4
  5.1 0.7 %copy-done.4 = s32[1,4,64]{2,1,0:T(4,128)S(1)} copy-done((s32[1,4,64]{2,1,0:T(4,128)S(1)}, s32[1,4,64]{2,1,0:T(4,128)}, u32[]{:S(2)}) %copy-start.4) | copy-done | bytes 1048
  5.8 44.1 %shard_map.85 = (bf16[512,128]{1,0:T(8,128)(2,1)S(1)}, bf16[512,128]{1,0:T(8,128)(2,1)S(1)}, bf16[3584,128]{1,0:T(8,128)(2,1)S(1)}) custom-call(bf16[512,128]{1,0:T(8,128)(2,1)S(1)} %copy-done.1, bf16[3456,128]{1,0:T(8,128)(2,1)S(1)} %bitcast.3, bf16[512,128]{1,0:T(8,128)(2,1)S(1)} %copy-done.2, s32[1]{0:T(128)S(6)} %copy.11.cnt_ref, ...), custom_call_target="tpu_custom_call" | custom-call | tf_op jit(solution)/shard_map/pallas_call | solution.py:429
  49.9 0.1 slice.3
  50.0 1.4 %convert.1 = f32[27,128,128]{2,1,0:T(8,128)} convert(bf16[27,128,128]{2,1,0:T(8,128)(2,1)S(1)} %bitcast.4) | non-fusion elementwise | flops 442368 | bytes 2654208 | tf_op jit(solution)/shard_map/reshape | solution.py:475
  51.4 0.7 %copy.12 = bf16[512,128]{1,0:T(8,128)(2,1)} copy(bf16[512,128]{1,0:T(8,128)(2,1)S(1)} %get-tuple-element.12) | data formatting | bytes 262144
  52.0 0.7 %copy.13 = bf16[512,128]{1,0:T(8,128)(2,1)} copy(bf16[512,128]{1,0:T(8,128)(2,1)S(1)} %get-tuple-element.13) | data formatting | bytes 262144
Async XLA Ops:
  1.3 1.2 %copy-start = (bf16[27,128,128]{2,1,0:T(8,128)(2,1)S(1)}, bf16[27,128,128]{2,1,0:T(8,128)(2,1)}, u32[]{:S(2)}) copy-start(bf16[27,128,128]{2,1,0:T(8,128)(2,1)} %param.7) | copy-start | bytes 2654212
  2.4 0.9 %copy-start.1 = (bf16[512,128]{1,0:T(8,128)(2,1)S(1)}, bf16[512,128]{1,0:T(8,128)(2,1)}, u32[]{:S(2)}) copy-start(bf16[512,128]{1,0:T(8,128)(2,1)} %x_ref.1) | copy-start | bytes 393220
  3.4 0.9 %copy-start.2 = (bf16[512,128]{1,0:T(8,128)(2,1)S(1)}, bf16[512,128]{1,0:T(8,128)(2,1)}, u32[]{:S(2)}) copy-start(bf16[512,128]{1,0:T(8,128)(2,1)} %cot_ref.1) | copy-start | bytes 393220
  4.3 0.8 %copy-start.3 = (s32[27,512]{1,0:T(8,128)S(1)}, s32[27,512]{1,0:T(8,128)}, u32[]{:S(2)}) copy-start(s32[27,512]{1,0:T(8,128)} %idx_ref.1) | copy-start | bytes 165892
  5.1 0.7 %copy-start.4 = (s32[1,4,64]{2,1,0:T(4,128)S(1)}, s32[1,4,64]{2,1,0:T(4,128)}, u32[]{:S(2)}) copy-start(s32[1,4,64]{2,1,0:T(4,128)} %exp_ref.1) | copy-start | bytes 3076

commit v2 on v1

--- a/solution.py
+++ b/solution.py
@@ -10,8 +10,9 @@
 BF = jnp.bfloat16
 F32 = jnp.float32
 MESH = pl.DeviceIdType.MESH
-PIECES = 2
 GROUP = 4
+SPAN = 4
+EARLY = 4
 
 
 def side_distance(slot_index):
@@ -26,17 +27,51 @@
     return near, chips // near
 
 
+def pieces_of(devices, padded_rows):
+    for pieces in (2,):
+        if padded_rows % (pieces * devices * 16) == 0:
+            return pieces
+    return 1
+
+
 def rows_each(devices, padded_rows):
-    share = -(-padded_rows // (PIECES * devices))
+    share = -(-padded_rows // (pieces_of(devices, padded_rows) * devices))
     return -(-share // 16) * 16
+
+
+def finish(
+    cuts, out_in, din_in, gw_in, out_ref, din_ref, gw_ref, rows, held, wide, row_in, row_out, in_sem, out_sem
+):
+    size = held.shape[0] // cuts
+    spans = [pl.ds(i * size, size) for i in range(cuts)]
+    fetch = [pltpu.make_async_copy(gw_in.at[s], held.at[s], in_sem.at[i]) for i, s in enumerate(spans)]
+    store = [pltpu.make_async_copy(wide.at[s], gw_ref.at[s], out_sem.at[i]) for i, s in enumerate(spans)]
+    into = [
+        pltpu.make_async_copy(source, rows.at[i], row_in.at[i]) for i, source in enumerate((out_in, din_in))
+    ]
+    away = [
+        pltpu.make_async_copy(rows.at[i], to, row_out.at[i]) for i, to in enumerate((out_ref, din_ref))
+    ]
+    for copy in fetch + into:
+        copy.start()
+    for i, s in enumerate(spans):
+        fetch[i].wait()
+        wide[s, :] = held[s, :].astype(F32)
+        store[i].start()
+    for i in range(2):
+        into[i].wait()
+        away[i].start()
+    for copy in store + away:
+        copy.wait()
 
 
 def kernel(
     n, r, offsets, padded,
-    x_ref, w_hbm, cot_ref, cnt_ref, idx_ref, exp_ref,
-    out_ref, din_ref, gw_ref,
+    x_hbm, w_hbm, cot_hbm, cnt_hbm, idx_hbm, exp_hbm,
+    out_hbm, din_hbm, gw_ref,
+    x_ref, cot_ref, idx_ref, exp_ref, out_ref, din_ref, in_sem, res_sem,
     w_s, idx_s, t01, t2, idxb, lob, lo16, iota_s, g_s, acc, d_s, r1, s2, r2, b_s, s3, r3, og,
-    hs, tacc, bs, br,
+    hs, tacc, bs, br, pre_s,
     w_sem, o_sem, hsem, hrem, bsem, brem,
     c1s, c1r, y1s, y1r, z1s, z1r, z2s, z2r, y2s, y2r, c2s, c2r,
 ):
@@ -50,6 +85,9 @@
     quarter = far * r
     half = near * quarter
     low = sites // 2
+    others = offsets - 1
+    middle = offsets // 2
+    PIECES = pieces_of(n, padded * ch)
     lo_rows = (sites + sides * halo) // 2
 
     def dev(cc, yy, zz):
@@ -76,12 +114,44 @@
         def _(owner=owner):
             pl.semaphore_signal(barrier, inc=1, device_id={"gx": owner}, device_id_type=MESH)
 
-    w_copy = pltpu.make_async_copy(w_hbm, w_s.at[pl.ds(0, offsets * ch)], w_sem)
-    w_copy.start()
+    w_copies = [
+        pltpu.make_async_copy(
+            w_hbm.at[pl.ds(source * ch, count * ch)], w_s.at[pl.ds(to * ch, count * ch)], w_sem.at[i]
+        )
+        for i, (source, to, count) in enumerate(
+            ((0, 0, middle), (middle + 1, middle, middle), (middle, others, 1))
+        )
+    ]
+    loads = [
+        pltpu.make_async_copy(source, to, in_sem.at[i])
+        for i, (source, to) in enumerate(
+            ((idx_hbm, idx_ref), (x_hbm, x_ref), (exp_hbm, exp_ref), (cot_hbm, cot_ref))
+        )
+    ]
+    for copy in loads + w_copies:
+        copy.start()
     w_s[pl.ds(offsets * ch, (padded - offsets) * ch), :] = jnp.zeros(
         ((padded - offsets) * ch, ch), BF
     )
 
+    loads[0].wait()
+    idx_s[...] = jnp.full(idx_s.shape, -1.0, F32)
+    idx_s[pl.ds(0, middle), :] = idx_ref[pl.ds(0, middle), :].astype(F32)
+    idx_s[pl.ds(middle, middle), :] = idx_ref[pl.ds(middle + 1, middle), :].astype(F32)
+    idx_s[pl.ds(others, 1), :] = idx_ref[pl.ds(middle, 1), :].astype(F32)
+    rows = idx_s[...]
+    lo_f = jnp.where(rows >= 2 * low, rows - 2 * low, jnp.where(rows >= low, rows - low, rows))
+    lo_b = jnp.where(
+        rows < 0, -1.0 * low + 1.0, jnp.where(rows >= lo_rows, rows - lo_rows, rows) - low / 2
+    )
+    rows_t = rows.T
+    lo_t = lo_f.T
+    for o in range(offsets):
+        idxb[o] = jnp.broadcast_to(rows_t[:, o : o + 1], (sites, ch))
+        lob[o] = jnp.broadcast_to(lo_t[:, o : o + 1], (sites, ch)).astype(BF)
+        lo16[o] = jnp.broadcast_to(lo_b[o : o + 1, :], (16, sites)).astype(BF)
+    loads[1].wait()
+    loads[2].wait()
     def export_picks(k):
         places = lax.broadcasted_iota(jnp.int32, (sites, halo), 0)
         return jnp.where(places == exp_ref[0, k : k + 1, :], 1.0, 0.0).astype(BF)
@@ -98,11 +168,6 @@
         @pl.when(jnp.logical_not(exists(me + side_distance(k))))
         def _(k=k):
             br[pl.ds(k * halo, halo), :] = jnp.zeros((halo, ch), BF)
-
-    greeted = len(fixed_peers)
-    for k in range(sides):
-        greeted += jnp.where(exists(me + side_distance(k)), 1, 0)
-    pl.semaphore_wait(barrier, greeted)
 
     def halo_copy(k):
         return pltpu.make_async_remote_copy(
@@ -124,27 +189,8 @@
             device_id_type=MESH,
         )
 
-    for k in range(sides):
-
-        @pl.when(exists(me + side_distance(k)))
-        def _(k=k):
-            halo_copy(k).start()
-
     t01[:, pl.ds(0, ch)] = x_ref[pl.ds(0, low), :]
     t01[:, pl.ds(ch, ch)] = x_ref[pl.ds(low, low), :]
-    idx_s[...] = jnp.full(idx_s.shape, -1.0, F32)
-    idx_s[pl.ds(0, offsets), :] = idx_ref[...].astype(F32)
-    rows = idx_s[...]
-    lo_f = jnp.where(rows >= 2 * low, rows - 2 * low, jnp.where(rows >= low, rows - low, rows))
-    lo_b = jnp.where(
-        rows < 0, -1.0 * low + 1.0, jnp.where(rows >= lo_rows, rows - lo_rows, rows) - low / 2
-    )
-    rows_t = rows.T
-    lo_t = lo_f.T
-    for o in range(padded):
-        idxb[o] = jnp.broadcast_to(rows_t[:, o : o + 1], (sites, ch))
-        lob[o] = jnp.broadcast_to(lo_t[:, o : o + 1], (sites, ch)).astype(BF)
-        lo16[o] = jnp.broadcast_to(lo_b[o : o + 1, :], (16, sites)).astype(BF)
     iota_s[...] = (
         lax.broadcasted_iota(jnp.int32, iota_s.shape, 0).astype(F32) - low / 2
     ).astype(BF)
@@ -160,9 +206,21 @@
             [jnp.where(lo == lanes_a, one, zero), jnp.where(lo == lanes_b, one, zero)], axis=1
         )
 
-    def own_rows(step, _):
-        for i in range(GROUP):
-            o = step * GROUP + i
+    live = jnp.where(idxb[others] >= 0, 1.0, 0.0)
+    g_s[:, pl.ds(others * ch, ch)] = (live * x_ref[...].astype(F32)).astype(BF)
+    g_s[:, pl.ds(offsets * ch, (padded - offsets) * ch)] = jnp.zeros(
+        (sites, (padded - offsets) * ch), BF
+    )
+
+    def each_span(rows, first, last):
+        whole = (last - first) // SPAN
+        lax.fori_loop(0, whole, lambda step, _: rows(first + step * SPAN, SPAN), 0)
+        if (last - first) % SPAN:
+            rows(first + whole * SPAN, (last - first) % SPAN)
+
+    def own_rows(start, count):
+        for i in range(count):
+            o = start + i
             both = jnp.dot(low_picks(o), t01[...], preferred_element_type=F32)
             place = idxb[o]
             picked = jnp.where(
@@ -171,45 +229,60 @@
             g_s[:, pl.ds(pl.multiple_of(o * ch, ch), ch)] = picked.astype(BF)
         return 0
 
-    lax.fori_loop(0, padded // GROUP, own_rows, 0)
-    w_copy.wait()
+    each_span(own_rows, 0, EARLY)
+    greeted = len(fixed_peers)
+    for k in range(sides):
+        greeted += jnp.where(exists(me + side_distance(k)), 1, 0)
+    pl.semaphore_wait(barrier, greeted)
+
+    for k in range(sides):
+
+        @pl.when(exists(me + side_distance(k)))
+        def _(k=k):
+            halo_copy(k).start()
+
+    each_span(own_rows, EARLY, others)
+    for copy in w_copies:
+        copy.wait()
     for k in range(sides):
 
         @pl.when(exists(me - side_distance(k)))
         def _(k=k):
             halo_copy(k).wait_recv()
 
-    acc[...] = jnp.zeros_like(acc)
-
-    def halo_rows(step, _):
-        for i in range(GROUP):
-            o = step * GROUP + i
+    acc[...] = jnp.dot(
+        g_s[:, pl.ds(others * ch, ch)], w_s[pl.ds(others * ch, ch), :], preferred_element_type=F32
+    )
+
+    def halo_rows(start, count):
+        for i in range(count):
+            o = start + i
             far_rows = jnp.dot(low_picks(o), t2[...], preferred_element_type=F32)
             where_o = pl.ds(pl.multiple_of(o * ch, ch), ch)
             g_s[:, where_o] = jnp.where(
                 idxb[o] >= 2 * low, far_rows, g_s[:, where_o].astype(F32)
             ).astype(BF)
-        span = pl.ds(pl.multiple_of(step * GROUP * ch, GROUP * ch), GROUP * ch)
+        span = pl.ds(pl.multiple_of(start * ch, ch), count * ch)
         acc[...] += jnp.dot(g_s[:, span], w_s[span, :], preferred_element_type=F32)
         return 0
 
-    lax.fori_loop(0, padded // GROUP, halo_rows, 0)
-
-    live = jnp.where(
-        lax.broadcasted_iota(jnp.int32, (sites, ch), 0) < cnt_ref[0], 1.0, 0.0
-    )
+    each_span(halo_rows, 0, others)
+    loads[3].wait()
+
     preact = acc[...]
     gate = jax.nn.sigmoid(preact)
     out_ref[...] = (live * (x_ref[...].astype(F32) + preact * gate)).astype(BF)
+    out_copy_rows = pltpu.make_async_copy(out_ref, out_hbm, res_sem.at[0])
+    out_copy_rows.start()
     pre_grad = (
         live * cot_ref[...].astype(F32) * gate * (1.0 + preact * (1.0 - gate))
     ).astype(BF)
-    acc[...] = pre_grad.astype(F32)
+    pre_s[...] = pre_grad
 
     def weight_rows(step, _):
         span = pl.ds(pl.multiple_of(step * GROUP * ch, GROUP * ch), GROUP * ch)
         d_s[span, :] = lax.dot_general(
-            g_s[:, span], acc[...].astype(BF), (((0,), (0,)), ((), ())),
+            g_s[:, span], pre_s[...], (((0,), (0,)), ((), ())),
             preferred_element_type=F32,
         )
         return 0
@@ -258,9 +331,21 @@
         part = at(p * piece + c * half, half)
         return remote(og.at[part], og.at[part], c2s.at[p], c2r.at[p], core_peer)
 
-    def out_copy(p):
-        part = pl.ds(p * piece, piece)
-        return pltpu.make_async_copy(og.at[part], gw_ref.at[part], o_sem.at[p])
+    def out_copies(p):
+        copies = []
+        for source, to, count in (
+            (0, 0, middle), (middle, middle + 1, middle), (others, middle, 1)
+        ):
+            first, last = max(source * ch, p * piece), min((source + count) * ch, (p + 1) * piece)
+            if first < last:
+                copies.append(
+                    pltpu.make_async_copy(
+                        og.at[pl.ds(first, last - first)],
+                        gw_ref.at[pl.ds(first + (to - source) * ch, last - first)],
+                        o_sem.at[3 * p + len(copies)],
+                    )
+                )
+        return copies
 
     def after_core(p):
         core_sum(p).wait_recv()
@@ -311,19 +396,19 @@
 
     def after_core_share(p):
         core_share(p).wait_recv()
-        out_copy(p).start()
+        for copy in out_copies(p):
+            copy.start()
 
     tacc[...] = jnp.zeros_like(tacc)
 
-    def table_rows(step, _):
-        span = pl.ds(pl.multiple_of(step * GROUP * ch, GROUP * ch), GROUP * ch)
+    def table_rows(start, count):
+        span = pl.ds(pl.multiple_of(start * ch, ch), count * ch)
         spread = lax.dot_general(
-            acc[...].astype(BF), w_s[span, :], (((1,), (1,)), ((), ())),
-            preferred_element_type=F32,
+            pre_s[...], w_s[span, :], (((1,), (1,)), ((), ())), preferred_element_type=F32
         )
         picks, parts = [], []
-        for i in range(GROUP):
-            o = step * GROUP + i
+        for i in range(count):
+            o = start + i
             upper = idxb[o] >= lo_rows
             term = spread[:, i * ch : (i + 1) * ch]
             parts.append(
@@ -341,50 +426,64 @@
         )
         return 0
 
+    def send_back():
+        bs[...] = tacc[pl.ds(lo_rows - sides * halo, sides * halo), pl.ds(ch, ch)].astype(BF)
+        for k in range(sides):
+
+            @pl.when(exists(me - side_distance(k)))
+            def _(k=k):
+                back_copy(k).start()
+
+    def finish_rows():
+        for k in range(sides):
+
+            @pl.when(exists(me + side_distance(k)))
+            def _(k=k):
+                back_copy(k).wait_recv()
+
+        scattered = lax.dot_general(
+            pre_s[...], w_s[pl.ds(others * ch, ch), :], (((1,), (1,)), ((), ())),
+            preferred_element_type=F32,
+        )
+        for k in range(sides):
+            scattered += jnp.dot(
+                export_picks(k), br[pl.ds(k * halo, halo), :], preferred_element_type=F32
+            )
+        own = jnp.concatenate(
+            [tacc[:, pl.ds(0, ch)], tacc[pl.ds(0, sites - lo_rows), pl.ds(ch, ch)]], axis=0
+        )
+        alive = jnp.where(idxb[others] >= 0, 1.0, 0.0)
+        din_ref[...] = (alive * (cot_ref[...].astype(F32) + own + scattered)).astype(BF)
+        pltpu.make_async_copy(din_ref, din_hbm, res_sem.at[1]).start()
+
     steps = padded // GROUP
-    first = -(-piece // (GROUP * ch))
-    lax.fori_loop(0, min(first, steps), weight_rows, 0)
-    core_sum(0).start()
-    lax.fori_loop(min(first, steps), steps, weight_rows, 0)
-    core_sum(1).start()
-    lax.fori_loop(0, 2, table_rows, 0)
-    after_core(0)
-    after_core(1)
-    lax.fori_loop(2, 4, table_rows, 0)
+    done = 0
+    for p in range(PIECES):
+        need = min(steps, -(-(p + 1) * piece // (GROUP * ch)))
+        if need > done:
+            lax.fori_loop(done, need, weight_rows, 0)
+            done = need
+        core_sum(p).start()
+    for p in range(PIECES):
+        after_core(p)
+    cuts = [min(others, cut) for cut in (12, 20, others)]
+    each_span(table_rows, 0, cuts[0])
     after_y(0)
-    lax.fori_loop(4, 6, table_rows, 0)
-    after_y(1)
-    lax.fori_loop(6, steps, table_rows, 0)
-    bs[...] = tacc[pl.ds(lo_rows - sides * halo, sides * halo), pl.ds(ch, ch)].astype(BF)
-    for k in range(sides):
-
-        @pl.when(exists(me - side_distance(k)))
-        def _(k=k):
-            back_copy(k).start()
-
-    after_z(0)
-    after_z(1)
+    each_span(table_rows, cuts[0], cuts[1])
+    for p in range(1, PIECES):
+        after_y(p)
+    each_span(table_rows, cuts[1], cuts[2])
+    send_back()
+    for p in range(PIECES):
+        after_z(p)
     after_z_share(0)
-    for k in range(sides):
-
-        @pl.when(exists(me + side_distance(k)))
-        def _(k=k):
-            back_copy(k).wait_recv()
-
-    scattered = jnp.dot(export_picks(0), br[pl.ds(0, halo), :], preferred_element_type=F32)
-    for k in range(1, sides):
-        scattered += jnp.dot(
-            export_picks(k), br[pl.ds(k * halo, halo), :], preferred_element_type=F32
-        )
-    own = jnp.concatenate(
-        [tacc[:, pl.ds(0, ch)], tacc[pl.ds(0, sites - lo_rows), pl.ds(ch, ch)]], axis=0
-    )
-    din_ref[...] = (live * (cot_ref[...].astype(F32) + own + scattered)).astype(BF)
-    after_z_share(1)
-    after_y_share(0)
-    after_y_share(1)
-    after_core_share(0)
-    after_core_share(1)
+    finish_rows()
+    for p in range(1, PIECES):
+        after_z_share(p)
+    for p in range(PIECES):
+        after_y_share(p)
+    for p in range(PIECES):
+        after_core_share(p)
 
     for k in range(sides):
 
@@ -405,7 +504,10 @@
             z_sum(p, k).wait_send()
             z_share(p, k).wait_send()
         core_share(p).wait_send()
-        out_copy(p).wait()
+        for copy in out_copies(p):
+            copy.wait()
+    out_copy_rows.wait()
+    pltpu.make_async_copy(din_ref, din_hbm, res_sem.at[1]).wait()
 
 
 def body(x, w, cot, counts, plan, exports):
@@ -414,28 +516,36 @@
     offsets = w.shape[0]
     padded = -(-offsets // GROUP) * GROUP
     sides, halo = exports.shape[1:]
+    middle = offsets // 2
     near, far = grid_of(n)
     r = rows_each(n, padded * ch)
     quarter = far * r
     half = near * quarter
-    total = PIECES * 2 * half
+    pieces = pieces_of(n, padded * ch)
+    total = pieces * 2 * half
     lo_rows = (sites + sides * halo) // 2
-    vmem = pl.BlockSpec(memory_space=pltpu.VMEM)
     anyspace = pl.BlockSpec(memory_space=pl.ANY)
-    smem = pl.BlockSpec(memory_space=pltpu.SMEM)
     dma = pltpu.SemaphoreType.DMA
-    y_slots = max(1, PIECES * (near - 1))
-    z_slots = max(1, PIECES * (far - 1))
+    y_slots = max(1, pieces * (near - 1))
+    z_slots = max(1, pieces * (far - 1))
     out, din, gw = pl.pallas_call(
         functools.partial(kernel, n, r, offsets, padded),
         out_shape=(
             jax.ShapeDtypeStruct((sites, ch), BF),
             jax.ShapeDtypeStruct((sites, ch), BF),
-            jax.ShapeDtypeStruct((total, ch), BF),
+            jax.ShapeDtypeStruct((offsets * ch, ch), BF),
         ),
-        in_specs=[vmem, anyspace, vmem, smem, vmem, vmem],
-        out_specs=(vmem, vmem, anyspace),
+        in_specs=[anyspace] * 6,
+        out_specs=(anyspace,) * 3,
         scratch_shapes=[
+            pltpu.VMEM((sites, ch), BF),
+            pltpu.VMEM((sites, ch), BF),
+            pltpu.VMEM((offsets, sites), jnp.int32),
+            pltpu.VMEM((1, sides, halo), jnp.int32),
+            pltpu.VMEM((sites, ch), BF),
+            pltpu.VMEM((sites, ch), BF),
+            dma((4,)),
+            dma((2,)),
             pltpu.VMEM((padded * ch, ch), BF),
             pltpu.VMEM((-(-padded // 8) * 8, sites), F32),
             pltpu.VMEM((sites // 2, 2 * ch), BF),
@@ -447,10 +557,10 @@
             pltpu.VMEM((sites, padded * ch), BF),
             pltpu.VMEM((sites, ch), F32),
             pltpu.VMEM((total, ch), F32),
-            pltpu.VMEM((PIECES * half, ch), F32),
+            pltpu.VMEM((pieces * half, ch), F32),
             pltpu.VMEM((y_slots * quarter, ch), BF),
             pltpu.VMEM((y_slots * quarter, ch), BF),
-            pltpu.VMEM((PIECES * quarter, ch), F32),
+            pltpu.VMEM((pieces * quarter, ch), F32),
             pltpu.VMEM((z_slots * r, ch), BF),
             pltpu.VMEM((z_slots * r, ch), BF),
             pltpu.VMEM((total, ch), BF),
@@ -458,22 +568,39 @@
             pltpu.VMEM((lo_rows, 2 * ch), F32),
             pltpu.VMEM((sides * halo, ch), BF),
             pltpu.VMEM((sides * halo, ch), BF),
-            dma,
-            dma((PIECES,)),
+            pltpu.VMEM((sites, ch), BF),
+            dma((3,)),
+            dma((3 * pieces,)),
             dma((sides,)), dma((sides,)), dma((sides,)), dma((sides,)),
-            dma((PIECES,)), dma((PIECES,)),
+            dma((pieces,)), dma((pieces,)),
             dma((y_slots,)), dma((y_slots,)),
             dma((z_slots,)), dma((z_slots,)),
             dma((z_slots,)), dma((z_slots,)),
             dma((y_slots,)), dma((y_slots,)),
-            dma((PIECES,)), dma((PIECES,)),
+            dma((pieces,)), dma((pieces,)),
         ],
         compiler_params=pltpu.CompilerParams(
-            collective_id=0, has_side_effects=True, vmem_limit_bytes=50 * 1024 * 1024
+            collective_id=0, has_side_effects=True, vmem_limit_bytes=60 * 1024 * 1024
         ),
     )(x, w.reshape(offsets * ch, ch), cot, counts, plan, exports)
-    grad_weight = gw[: offsets * ch].astype(F32).reshape(offsets, ch, ch)
-    return out, din, grad_weight
+    out, din, gw = pl.pallas_call(
+        functools.partial(finish, 3),
+        out_shape=(
+            jax.ShapeDtypeStruct((sites, ch), BF),
+            jax.ShapeDtypeStruct((sites, ch), BF),
+            jax.ShapeDtypeStruct((offsets * ch, ch), F32),
+        ),
+        in_specs=[anyspace] * 3,
+        out_specs=(anyspace,) * 3,
+        scratch_shapes=[
+            pltpu.VMEM((2, sites, ch), BF),
+            pltpu.VMEM((offsets * ch, ch), BF),
+            pltpu.VMEM((offsets * ch, ch), F32),
+            dma((2,)), dma((2,)), dma((3,)), dma((3,)),
+        ],
+        compiler_params=pltpu.CompilerParams(vmem_limit_bytes=60 * 1024 * 1024),
+    )(out, din, gw)
+    return out, din, gw.reshape(offsets, ch, ch)
 
 
 def solution(mesh):

time: 53 us -> 47 us (0.89)
  local copies, waits for them, and re-layouts: 5.86 us -> 0 us
  other arithmetic: 1.41 us -> 0 us
  Pallas kernels: 44.1 us -> 45.4 us
    unnamed x12 -> x0, local copies, waits for them, and re-layouts: 5.8 us -> none
    pallas_call x0 -> x1, Pallas kernels: none -> 2.37 us  [body(): pl.pallas_call(functools.partial(finish, 3), out_shape=(jax.ShapeDtypeStr...]
    reshape x1 -> x0, other arithmetic: 1.41 us -> none  [body(): grad_weight = gw[:offsets * ch].astype(F32).reshape(offsets, ch, ch)]
    pallas_call x1, Pallas kernels: 44.1 us -> 43.1 us  [body(): pl.pallas_call(functools.partial(kernel, n, r, offsets, padded), out_shap...]
where the time goes in v2:
time: 47 us; the launch traced here: 46.7 us
  Pallas kernels  45.4 us (97%)
  between operations  1.29 us (3%)
    pallas_call x1, Pallas kernels, body(): pl.pallas_call(functools.partial(kernel, n, r, offsets, padded), out_shap...  43.1 us
    pallas_call x1, Pallas kernels, body(): pl.pallas_call(functools.partial(finish, 3), out_shape=(jax.ShapeDtypeStr...  2.37 us

profile of v2, /device:TPU:1, one launch (start us, length us, event | category | flops | bytes accessed | tf_op | source)
XLA Modules:
  0.0 46.7 jit_solution(13696888474293230631)
XLA Ops:
  1.3 43.1 %shard_map.85 = (bf16[512,128]{1,0:T(8,128)(2,1)}, bf16[512,128]{1,0:T(8,128)(2,1)}, bf16[3456,128]{1,0:T(8,128)(2,1)}) custom-call(bf16[512,128]{1,0:T(8,128)(2,1)} %x_hbm.1, bf16[3456,128]{1,0:T(8,128)(2,1)} %bitcast.2, bf16[512,128]{1,0:T(8,128)(2,1)} %cot_hbm.1, s32[1]{0:T(128)S(6)} %copy.9.cnt_hbm, s32[27,512]{1,0:T(8,128)} %idx_hbm.1, s32[1,4,64]{2,1,0:T(4,128)} %exp_hbm.1), custom_call_target="tpu_custom_call" | custom-call | tf_op jit(solution)/shard_map/pallas_call | solution.py:531
  44.3 2.4 %shard_map.86 = (bf16[512,128]{1,0:T(8,128)(2,1)}, bf16[512,128]{1,0:T(8,128)(2,1)}, f32[3456,128]{1,0:T(8,128)}) custom-call(bf16[512,128]{1,0:T(8,128)(2,1)} %get-tuple-element.9.out_in, bf16[512,128]{1,0:T(8,128)(2,1)} %get-tuple-element.10.din_in, bf16[3456,128]{1,0:T(8,128)(2,1)} %get-tuple-element.11.gw_in), custom_call_target="tpu_custom_call" | custom-call | tf_op jit(solution)/shard_map/pallas_call | solution.py:586

commit v3 on v2

--- a/solution.py
+++ b/solution.py
@@ -12,7 +12,6 @@
 MESH = pl.DeviceIdType.MESH
 GROUP = 4
 SPAN = 4
-EARLY = 4
 
 
 def side_distance(slot_index):
@@ -212,11 +211,11 @@
         (sites, (padded - offsets) * ch), BF
     )
 
-    def each_span(rows, first, last):
-        whole = (last - first) // SPAN
-        lax.fori_loop(0, whole, lambda step, _: rows(first + step * SPAN, SPAN), 0)
-        if (last - first) % SPAN:
-            rows(first + whole * SPAN, (last - first) % SPAN)
+    def each_span(rows, first, last, span=SPAN):
+        whole = (last - first) // span
+        lax.fori_loop(0, whole, lambda step, _: rows(first + step * span, span), 0)
+        if (last - first) % span:
+            rows(first + whole * span, (last - first) % span)
 
     def own_rows(start, count):
         for i in range(count):
@@ -229,7 +228,6 @@
             g_s[:, pl.ds(pl.multiple_of(o * ch, ch), ch)] = picked.astype(BF)
         return 0
 
-    each_span(own_rows, 0, EARLY)
     greeted = len(fixed_peers)
     for k in range(sides):
         greeted += jnp.where(exists(me + side_distance(k)), 1, 0)
@@ -241,7 +239,7 @@
         def _(k=k):
             halo_copy(k).start()
 
-    each_span(own_rows, EARLY, others)
+    each_span(own_rows, 0, others)
     for copy in w_copies:
         copy.wait()
     for k in range(sides):
@@ -266,7 +264,7 @@
         acc[...] += jnp.dot(g_s[:, span], w_s[span, :], preferred_element_type=F32)
         return 0
 
-    each_span(halo_rows, 0, others)
+    each_span(halo_rows, 0, others, 13 if others % 13 == 0 else SPAN)
     loads[3].wait()
 
     preact = acc[...]

time: 47 us -> 46.6 us (level)
  Pallas kernels: 45.4 us -> 44.8 us
    pallas_call x1, Pallas kernels: 43.1 us -> 42.4 us  [body(): pl.pallas_call(functools.partial(kernel, n, r, offsets, padded), out_shap...]
where the time goes in v3:
time: 46.6 us; the launch traced here: 46.1 us
  Pallas kernels  44.8 us (96%)
  between operations  1.29 us (3%)
    pallas_call x1, Pallas kernels, body(): pl.pallas_call(functools.partial(kernel, n, r, offsets, padded), out_shap...  42.4 us
    pallas_call x1, Pallas kernels, body(): pl.pallas_call(functools.partial(finish, 3), out_shape=(jax.ShapeDtypeStr...  2.37 us

profile of v3, /device:TPU:1, one launch (start us, length us, event | category | flops | bytes accessed | tf_op | source)
XLA Modules:
  0.0 46.1 jit_solution(2222031021830131969)
XLA Ops:
  1.3 42.4 %shard_map.85 = (bf16[512,128]{1,0:T(8,128)(2,1)}, bf16[512,128]{1,0:T(8,128)(2,1)}, bf16[3456,128]{1,0:T(8,128)(2,1)}) custom-call(bf16[512,128]{1,0:T(8,128)(2,1)} %x_hbm.1, bf16[3456,128]{1,0:T(8,128)(2,1)} %bitcast.2, bf16[512,128]{1,0:T(8,128)(2,1)} %cot_hbm.1, s32[1]{0:T(128)S(6)} %copy.9.cnt_hbm, s32[27,512]{1,0:T(8,128)} %idx_hbm.1, s32[1,4,64]{2,1,0:T(4,128)} %exp_hbm.1), custom_call_target="tpu_custom_call" | custom-call | tf_op jit(solution)/shard_map/pallas_call | solution.py:529
  43.7 2.4 %shard_map.86 = (bf16[512,128]{1,0:T(8,128)(2,1)}, bf16[512,128]{1,0:T(8,128)(2,1)}, f32[3456,128]{1,0:T(8,128)}) custom-call(bf16[512,128]{1,0:T(8,128)(2,1)} %get-tuple-element.9.out_in, bf16[512,128]{1,0:T(8,128)(2,1)} %get-tuple-element.10.din_in, bf16[3456,128]{1,0:T(8,128)(2,1)} %get-tuple-element.11.gw_in), custom_call_target="tpu_custom_call" | custom-call | tf_op jit(solution)/shard_map/pallas_call | solution.py:584
